TPU v7x, 512 devices: a whole 4x8x8 slice. The times are simulated.
512 devices in a mesh: space: 32 (over y_hi, z, core), tm: 16 (over y_lo, x).
Axes of the slice: x: 4, y: 8 (y_hi: 2, y_lo: 4; y = y_hi * 4 + y_lo), z: 8, core: 2. Of those that a mesh axis runs over, the one named last changes fastest.
Arguments:
- video_slab: float32 [256, 512, 2048], P('space', None, 'tm'), may hold values from -6 to 6
- first_cols: float32 [512, 160], replicated, may hold values from -0.25 to 0.25
- first_frames: float32 [2048, 160], P('tm'), may hold values from -0.125 to 0.125
- second_rows: float32 [256, 160], P('space'), may hold values from -0.375 to 0.375
- second_frames: float32 [2048, 160], P('tm'), may hold values from -0.125 to 0.125
- third_rows: float32 [256, 96], P('space'), may hold values from -0.375 to 0.375
- third_cols: float32 [512, 96], replicated, may hold values from -0.25 to 0.25
- core_rows: float32 [256, 320], replicated, may hold values from -0.375 to 0.375
- core_cols: float32 [512, 320], replicated, may hold values from -0.25 to 0.25
- core_frames: float32 [2048, 192], P('tm'), may hold values from -0.125 to 0.125
Outputs:
- sketch_rows: float32 [256, 160], P('space')
- sketch_cols: float32 [512, 160], P('space')
- sketch_frames: float32 [2048, 96], P('tm')
- core_sketch: float32 [320, 320, 192], P(None, 'space', 'tm')
All inputs are finite; a program needn't handle non-finite values.
Results may differ from a plain program's by a relative error of at most 0.0001.
Values sent between devices are 32-bit elements; how exact they have to be, the bound alone decides.
A program may use at most 64 MiB of HBM per device.

v0:
```python
import jax
import jax.numpy as jnp
from jax import lax
from jax.sharding import PartitionSpec as P

highest = lax.Precision.HIGHEST


def per_device(
    video_slab,
    first_cols,
    first_frames,
    second_rows,
    second_frames,
    third_rows,
    third_cols,
    core_rows,
    core_cols,
    core_frames,
):
    first_width = first_cols.shape[1]
    third_width = third_cols.shape[1]
    stacked = jnp.concatenate([first_cols, third_cols, core_cols], axis=1)
    through = jnp.einsum("ijt,jc->itc", video_slab, stacked, precision=highest)
    first_part = through[:, :, :first_width]
    third_part = through[:, :, first_width : first_width + third_width]
    core_inner = through[:, :, first_width + third_width :]
    row_term = jnp.einsum("itr,tr->ir", first_part, first_frames, precision=highest)
    frame_term = jnp.einsum("itr,ir->tr", third_part, third_rows, precision=highest)
    col_frames = jnp.einsum("ijt,tr->ijr", video_slab, second_frames, precision=highest)
    col_term = jnp.einsum("ijr,ir->jr", col_frames, second_rows, precision=highest)
    sketch_frames = lax.psum(frame_term, "space")
    sketch_rows, summed = lax.psum((row_term, col_term), "tm")
    sketch_cols = lax.psum_scatter(summed, "space", scatter_dimension=0, tiled=True)
    arrived = lax.all_to_all(core_inner, "space", split_axis=2, concat_axis=0, tiled=True)
    blended = jnp.einsum("itb,ia->atb", arrived, core_rows, precision=highest)
    partial_value = jnp.einsum("atb,tc->abc", blended, core_frames, precision=highest)
    core_sketch = lax.psum_scatter(partial_value, "tm", scatter_dimension=2, tiled=True)
    return (sketch_rows, sketch_cols, sketch_frames, core_sketch)


def solution(mesh):
    return jax.shard_map(
        per_device,
        mesh=mesh,
        in_specs=(
            P("space", None, "tm"),
            P(),
            P("tm", None),
            P("space", None),
            P("tm", None),
            P("space", None),
            P(),
            P(),
            P(),
            P("tm", None),
        ),
        out_specs=(P("space", None), P("space", None), P("tm", None), P(None, "space", "tm")),
        check_vma=False,
    )
```

profile of v0, /device:TPU:32, one launch (start us, length us, event | category | flops | bytes accessed | tf_op | source)
XLA Modules:
  0.0 335.2 jit_solution(17374778441122667771)
XLA Ops:
  8.0 1.6 copy-done
  9.6 5.3 %convolution_bitcast_fusion = f32[8,128,576]{1,2,0:T(8,128)S(1)} fusion(f32[8,512,128]{2,1,0:T(8,128)S(1)} %copy-done, f32[512,320]{0,1:T(8,128)} %param.18, f32[512,96]{0,1:T(8,128)} %param.16, f32[512,160]{0,1:T(8,128)} %param.11), kind=kOutput, calls=%fused_computation.1 | convolution fusion | flops 3624468480 | bytes 5636096 | tf_op jit(solution)/shard_map/ijt,jc->itc/dot_general | solution.py:24
  14.9 1.4 copy-done.1
  16.3 0.1 slice.14
  16.4 1.8 copy.16
  18.2 16.0 %all-to-all-start = ((f32[8,128,320]{1,0,2:T(8,128)}), f32[8,128,320]{1,0,2:T(8,128)S(1)}, u32[]{:S(2)}, u32[]{:S(2)}) async-start(f32[8,128,320]{1,0,2:T(8,128)} %copy.16), calls=%async_computation | async-start | bytes 2621440 | tf_op jit(solution)/shard_map/all_to_all | solution.py:35
  34.2 0.0 reduce-scatter.3.cloned.1.call-start
  34.3 3.2 multiply_reduce_fusion
  37.5 2.0 copy.27
  39.5 0.0 reduce-scatter.3.cloned.1.call-update
  39.5 0.2 all-reduce.4.cloned.1.call-start
  39.8 26.6 %all-to-all-done = f32[8,128,320]{1,0,2:T(8,128)S(1)} async-done(((f32[8,128,320]{1,0,2:T(8,128)}), f32[8,128,320]{1,0,2:T(8,128)S(1)}, u32[]{:S(2)}, u32[]{:S(2)}) %all-to-all-start) | async-done | bytes 1310752 | tf_op jit(solution)/shard_map/all_to_all | solution.py:35
  66.3 2.6 fusion.2
  68.9 4.1 %fusion = f32[320,10,192]{0,2,1:T(8,128)} fusion(f32[128,10,320]{0,2,1:T(8,128)S(1)} %fusion.2, f32[128,192]{0,1:T(8,128)S(1)} %copy-done.2), kind=kOutput, calls=%fused_computation.2 | convolution fusion | flops 943718400 | bytes 4194304 | tf_op jit(solution)/shard_map/atb,tc->abc/dot_general | solution.py:37
  73.0 0.0 all-reduce.4.cloned.1.call-update
  73.1 1.0 slice-done
  74.1 1.5 fusion.9
  75.6 0.1 copy.20
  75.7 0.1 copy.29
  75.8 1.3 dynamic-slice
  77.7 1.0 fusion.11
  78.7 169.6 %psum.23 = f32[128,96]{0,1:T(8,128)} all-reduce(f32[128,96]{0,1:T(8,128)S(1)} %bitcast.49), channel_id=1, replica_groups=mesh['space'=32,'tm'=16] {'space'}, use_global_device_ids=true, to_apply=%region_3.0 | all-reduce | flops 12288 | bytes 98304 | tf_op jit(solution)/shard_map/psum | solution.py:32
  248.3 77.8 %all-reduce.1 = (f32[8,160]{1,0:T(8,128)}, f32[16,160]{1,0:T(8,128)}) all-reduce(f32[8,160]{1,0:T(8,128)S(1)} %bitcast.51, f32[16,160]{1,0:T(8,128)} %reduce-scatter.3.cloned.1.call-done), channel_id=1, replica_groups=mesh['space'=32,'tm'=16] {'tm'}, use_global_device_ids=true, to_apply=%region_0.0 | all-reduce | flops 3840 | bytes 30720 | tf_op jit(solution)/shard_map/psum | solution.py:33
  326.1 1.7 constant_dynamic-slice_fusion
  (17 shorter events, 0.0 us)
Async XLA Ops:
  8.0 1.6 copy-start
  14.9 1.4 copy-start.1
  18.2 16.0 %copy-start.3 = (f32[128,160]{0,1:T(8,128)S(1)}, f32[128,160]{0,1:T(8,128)}, u32[]{:S(2)}) copy-start(f32[128,160]{0,1:T(8,128)} %param.14) | copy-start | bytes 245764
  18.2 16.1 %copy-start.5 = (f32[8,160]{1,0:T(8,128)S(1)}, f32[8,160]{1,0:T(8,128)}, u32[]{:S(2)}) copy-start(f32[8,160]{1,0:T(8,128)} %param.13) | copy-start | bytes 15364
  18.2 48.1 %all-to-all-start = ((f32[8,128,320]{1,0,2:T(8,128)}), f32[8,128,320]{1,0,2:T(8,128)S(1)}, u32[]{:S(2)}, u32[]{:S(2)}) async-start(f32[8,128,320]{1,0,2:T(8,128)} %copy.16), calls=%async_computation | async-start | bytes 2621440 | tf_op jit(solution)/shard_map/all_to_all | solution.py:35
  34.2 214.1 %reduce-scatter.3.cloned.1.call-start = ((), (), s32[]{:S(2)}) async-start(), calls=%async_computation.2 | async-start | bytes 540672 | tf_op jit(solution)/shard_map/reduce_scatter | solution.py:34
  39.5 286.6 %all-reduce.4.cloned.1.call-start = ((), (), s32[]{:S(2)}) async-start(), calls=%async_computation.3 | async-start | bytes 5898240
  66.3 2.6 copy-start.2
  73.0 1.1 slice-start
  73.0 1.1 copy-start.4
  73.1 2.6 copy-start.6
  73.1 4.6 %slice-start.1 = ((f32[8,128,576]{1,2,0:T(8,128)}), f32[8,128,96]{1,2,0:T(8,128)S(1)}, s32[]{:S(2)}) async-start(f32[8,128,576]{1,2,0:T(8,128)} %copy-done.1), calls=%async_computation.5 | async-start | bytes 786432 | tf_op jit(solution)/shard_map/slice | solution.py:26
Sparse Core Ops, SparseCore 0:
  39.6 124.4 reduce-scatter.2
Sparse Core Ops, SparseCore 1:
  73.1 177.9 all-reduce.3
where the time goes:
time: 336 us; the launch traced here: 335 us
  blocking collectives  247 us (74%)
  waiting for transfers between devices  26.6 us (8%)
  matrix products  17.6 us (5%)
  between operations  16.3 us (5%)
  starting transfers between devices  16.2 us (5%)
  local copies, waits for them, and re-layouts  11.1 us (3%)
    psum x1, blocking collectives, per_device(): sketch_frames = lax.psum(frame_term, 'space')  170 us
    psum x1, blocking collectives, per_device(): sketch_rows, summed = lax.psum((row_term, col_term), 'tm')  77.8 us
    all_to_all x1, waiting for transfers between devices, per_device(): lax.all_to_all(core_inner, 'space', split_axis=2, concat_axis=0, tiled=True)  26.6 us
    all_to_all x1, starting transfers between devices, per_device(): lax.all_to_all(core_inner, 'space', split_axis=2, concat_axis=0, tiled=True)  16 us
  transfers between devices with their start and end apart: 3, of which 1 were waited for; matrix products, arithmetic and copies ran while one was open for 5% of the time, Pallas kernels for 0%

commit v1 on v0

v1 whole, which is shorter than its diff:
```python
import functools

import jax
import jax.numpy as jnp
from jax import lax
from jax.experimental import pallas as pl
from jax.experimental.pallas import tpu as pltpu
from jax.sharding import PartitionSpec as P

MESH = pl.DeviceIdType.MESH
f32, bf16 = jnp.float32, jnp.bfloat16

NN = (((1,), (0,)), ((), ()))
NT = (((1,), (1,)), ((), ()))
TN = (((0,), (0,)), ((), ()))


def dot(a, b, dims=NN):
    return lax.dot_general(a, b, dims, preferred_element_type=f32)


def halves(a):
    high = a.astype(bf16)
    return high, (a - high.astype(f32)).astype(bf16)


def kernel(
    slab_given, first_cols_given, third_cols_given, core_cols_given, first_frames_given, second_frames_given,
    core_frames_given, second_rows_given, third_rows_given, core_rows_given,
    out_rows, out_cols, out_frames, out_core,
    slab, first_cols, third_cols, core_cols, first_frames, second_frames, core_frames, second_rows, third_rows, core_rows,
    order, cols_hi, cols_lo, frames_hi, frames_lo, rows_hi, rows_lo, split, inner, folded_hi, folded_lo, second_hi, second_lo, third_wide,
    part, far, near, after, pair_in, cross_in, tiles, gathered,
    small, core_in, layer_out, layer_in, frame_part, frame_in, frame_layer, frame_other, frame_last,
    line_out, line_in, ring_out, ring_in,
    load_sem, send_sem, recv_sem, send_space, recv_space, send_layer, recv_layer, send_line, recv_line, send_ring, recv_ring,
):
    space, tm = lax.axis_index("space"), lax.axis_index("tm")
    y_hi, z, core = space // 16, lax.rem(space // 2, 8), lax.rem(space, 2)
    y_lo, x = tm // 4, lax.rem(tm, 4)
    y = y_hi * 4 + y_lo

    def at_x(other):
        return (space, y_lo * 4 + other)

    def at_y(other):
        return (lax.rem(other // 4, 2) * 16 + z * 2 + core, lax.rem(other, 4) * 4 + x)

    def at_z(other):
        return (y_hi * 16 + other * 2 + core, tm)

    def load(number, source, target):
        return pltpu.make_async_copy(source, target, load_sem.at[number])

    def load_pair(pair):
        rows = pl.ds(2 * pair, 2)
        return load(pair, slab_given.at[rows], slab.at[rows])

    loads = {
        "core_cols": load(4, core_cols_given, core_cols),
        "first_cols": load(5, first_cols_given, first_cols),
        "third_cols": load(6, third_cols_given, third_cols),
        "core_frames": load(7, core_frames_given, core_frames),
        "second_rows": load(8, second_rows_given, second_rows),
        "third_rows": load(9, third_rows_given, third_rows),
        "second_frames": load(10, second_frames_given, second_frames),
        "first_frames": load(11, first_frames_given, first_frames),
        "core_rows": load(12, core_rows_given, core_rows),
    }
    for each in ("core_cols", "first_cols", "third_cols"):
        loads[each].start()
    for pair in range(4):
        load_pair(pair).start()
    for each in ("core_frames", "second_rows", "third_rows", "second_frames", "first_frames", "core_rows"):
        loads[each].start()

    barrier = pltpu.get_barrier_semaphore()

    def greet(device):
        pl.semaphore_signal(barrier, inc=1, device_id=device, device_id_type=MESH)

    @pl.loop(1, 32)
    def _(step):
        greet((lax.rem(space + step, 32), tm))

    for step in (1, 2, 3):
        greet(at_x(lax.rem(x + step, 4)))
        for flip in (0, 16):
            greet((lax.rem(space + flip, 32), lax.rem(y_lo + step, 4) * 4 + x))

    loads["core_cols"].wait()
    loads["first_cols"].wait()
    loads["third_cols"].wait()
    loads["core_frames"].wait()
    hi, lo = halves(first_cols[...])
    cols_hi[0:160, :], cols_lo[0:160, :] = hi, lo
    hi, lo = halves(third_cols[...])
    cols_hi[160:256, :], cols_lo[160:256, :] = hi, lo
    for quarter in range(4):
        lanes = slice(128 * quarter, 128 * quarter + 128)
        order[quarter] = core_cols[:, lanes]
        for place in range(10):
            hi, lo = halves(order[quarter, pl.ds(place, 32, stride=10), :])
            rows = slice(256 + 32 * place, 288 + 32 * place)
            cols_hi[rows, lanes], cols_lo[rows, lanes] = hi, lo

    for other in range(4):
        for place in range(4):
            line = (place % 2) * 2 + place // 2
            base = 12 * (line * 4 + other)
            row = 24 * (other * 4 + place)
            eight = core_frames[base : base + 8, :]
            four = core_frames[base + 8 : base + 12, :]
            blank = jnp.zeros((8, 128), f32)
            blank4 = jnp.zeros((4, 128), f32)
            block = jnp.concatenate(
                [
                    jnp.concatenate([eight, blank], axis=1),
                    jnp.concatenate([blank, eight], axis=1),
                    jnp.concatenate([four, blank4], axis=1),
                    jnp.concatenate([blank4, four], axis=1),
                ],
                axis=0,
            )
            hi, lo = halves(block)
            frames_hi[row : row + 24, :], frames_lo[row : row + 24, :] = hi, lo

    def columns(pair):
        load_pair(pair).wait()
        lanes = pl.ds(pl.multiple_of(pair * 256, 256), 256)
        low_lanes = pl.ds(pl.multiple_of(pair * 256 + 1024, 256), 256)
        block = jnp.concatenate([slab[2 * pair], slab[2 * pair + 1]], axis=1)
        hi, lo = halves(block)
        split[:, lanes] = hi
        split[:, low_lanes] = lo
        product = dot(cols_hi[...], hi) + dot(cols_hi[...], lo) + dot(cols_lo[...], hi)
        inner[pair] = product[0:256, :]
        hi, lo = halves(product[256:576, :].reshape(2, 5, 32, 256))
        chunk = pair // 2
        for row in range(2):
            place = 2 * lax.rem(pair, 2) + row
            for half in range(2):
                folded_hi[chunk, :, place, :, half * 128 : half * 128 + 128] = hi[half, :, :, row * 128 : row * 128 + 128]
                folded_lo[chunk, :, place, :, half * 128 : half * 128 + 128] = lo[half, :, :, row * 128 : row * 128 + 128]

    def frames(chunk):
        right_hi = folded_hi[chunk].reshape(640, 256)
        right_lo = folded_lo[chunk].reshape(640, 256)
        product = (
            dot(frames_hi[...], right_hi, NT) + dot(frames_hi[...], right_lo, NT) + dot(frames_lo[...], right_hi, NT)
        )
        part[chunk] = product.reshape(4, 2, 2, 24, 640)

    def copy(source, target, number, device):
        return pltpu.make_async_remote_copy(
            src_ref=source, dst_ref=target, send_sem=send_sem.at[number], recv_sem=recv_sem.at[number],
            device_id=device, device_id_type=MESH,
        )

    right, left, across = lax.rem(x + 1, 4), lax.rem(x + 3, 4), lax.rem(x + 2, 4)
    ways = ((right, left), (left, right))

    @pl.loop(0, 2)
    def _(pair):
        columns(pair)

    frames(0)
    pl.semaphore_wait(barrier, 40)
    sent = []

    def begin(chunk):
        onward, back = ways[chunk]
        first = copy(part.at[chunk, across], far.at[chunk], 3 * chunk, at_x(onward))
        second = copy(part.at[chunk, back], near.at[chunk], 3 * chunk + 1, at_x(back))
        first.start()
        second.start()
        sent.extend([first, second])
        return first, second

    def relay(chunk, first):
        onward, _ = ways[chunk]
        first.wait_recv()
        part[chunk, onward] += far[chunk]
        third = copy(part.at[chunk, onward], after.at[chunk], 3 * chunk + 2, at_x(onward))
        third.start()
        sent.append(third)
        return third

    ring = [begin(0)]

    @pl.loop(2, 4)
    def _(pair):
        columns(pair)

    frames(1)
    ring.append(begin(1))

    index_k = lax.broadcasted_iota(jnp.int32, (8, 1024), 0)
    index_l = lax.broadcasted_iota(jnp.int32, (8, 1024), 1) // 128
    spread = (index_k == index_l).astype(f32)

    for each in ("second_rows", "third_rows", "second_frames", "first_frames", "core_rows"):
        loads[each].wait()

    def widen(values):
        return lax.dot_general(values, spread, TN, precision=lax.Precision.HIGHEST, preferred_element_type=f32)

    wide_second = widen(second_rows[...])
    for row in range(8):
        lanes = slice(row * 128, row * 128 + 128)
        value = second_frames[...] * wide_second[:, lanes]
        hi, lo = halves(value)
        second_hi[0:128, lanes], second_lo[0:128, lanes] = hi[0:128], lo[0:128]
        for copies in range(4):
            rows = slice(128 + 32 * copies, 160 + 32 * copies)
            second_hi[rows, lanes], second_lo[rows, lanes] = hi[128:160], lo[128:160]
    third_wide[...] = widen(third_rows[...])

    relayed = [relay(0, ring[0][0])]

    second = (
        dot(split[:, 0:1024], second_hi[...], NT)
        + dot(split[:, 1024:2048], second_hi[...], NT)
        + dot(split[:, 0:1024], second_lo[...], NT)
    )
    main = second[:, 0:128].reshape(2, 8, 2, 16, 128)
    tail = second[:, 128:256].reshape(2, 8, 2, 2, 8, 128)
    quarter = lax.broadcasted_iota(jnp.int32, (8, 8, 128), 2) // 32
    for which in range(2):
        small[which, :, 0:16, :] = main[0, :, which]
        small[which, :, 16:32, :] = main[1, :, which]
        small[which, :, 32:40, :] = jnp.where(
            quarter < 2,
            jnp.where(quarter == 0, tail[0, :, which, 0], tail[0, :, which, 1]),
            jnp.where(quarter == 2, tail[1, :, which, 0], tail[1, :, which, 1]),
        )

    total = jnp.zeros((96, 128), f32)
    for row in range(8):
        place = slice((row % 2) * 128, (row % 2) * 128 + 128)
        total = total + inner[row // 2, 160:256, place] * third_wide[:, row * 128 : row * 128 + 128]
    frame_part[...] = total.reshape(2, 48, 128)

    other_core = (y_hi * 16 + z * 2 + 1 - core, tm)
    swap = copy(small.at[1 - core], core_in, 6, other_core)
    swap.start()
    swap_frames = copy(frame_part.at[1 - core], frame_in, 7, other_core)
    swap_frames.start()
    sent.extend([swap, swap_frames])

    relayed.append(relay(1, ring[1][0]))

    rows_total = jnp.zeros((16, 160), f32)
    index_k = lax.broadcasted_iota(jnp.int32, (16, 256), 0)
    index_l = lax.broadcasted_iota(jnp.int32, (16, 256), 1) // 128
    for pair in range(4):
        value = inner[pair, 0:160, :] * jnp.concatenate([first_frames[...], first_frames[...]], axis=1)
        hi, lo = halves(value)
        ones = (index_k == index_l + 2 * pair).astype(f32).astype(bf16)
        rows_total = rows_total + dot(ones, hi, NT) + dot(ones, lo, NT)

    hi, lo = halves(core_rows[...])
    rows_hi[...], rows_lo[...] = hi, lo

    swap.wait_recv()
    layer_out[...] = small[core] + core_in[...]
    swap_frames.wait_recv()
    frame_layer[z] = frame_part[core] + frame_in[...]

    def layer_copy(other, slot, kind):
        if kind == 0:
            source, target = layer_out.at[other], layer_in.at[slot]
        else:
            source, target = frame_layer.at[z], frame_layer.at[slot]
        return pltpu.make_async_remote_copy(
            src_ref=source, dst_ref=target, send_sem=send_layer.at[kind, other], recv_sem=recv_layer.at[kind, slot],
            device_id=at_z(other), device_id_type=MESH,
        )

    @pl.loop(1, 8)
    def _(step):
        other = lax.rem(z + step, 8)
        layer_copy(other, z, 0).start()
        layer_copy(other, z, 1).start()

    layer_in[z] = layer_out[z]

    def pair_stage(chunk):
        ring[chunk][1].wait_recv()
        relayed[chunk].wait_recv()
        part[chunk, x] = part[chunk, x] + near[chunk] + after[chunk]
        step = copy(
            part.at[chunk, x, 1 - lax.rem(y_lo, 2)], pair_in.at[chunk], 8 + chunk,
            (space, (y_lo + 1 - 2 * lax.rem(y_lo, 2)) * 4 + x),
        )
        step.start()
        sent.append(step)
        return step

    def cross_stage(chunk, step):
        step.wait_recv()
        mine = lax.rem(y_lo, 2)
        part[chunk, x, mine] = part[chunk, x, mine] + pair_in[chunk]
        cross = copy(
            part.at[chunk, x, mine, 1 - y_lo // 2], cross_in.at[chunk], 10 + chunk,
            (space, lax.rem(y_lo + 2, 4) * 4 + x),
        )
        cross.start()
        sent.append(cross)
        return cross

    pairs = [pair_stage(0)]

    @pl.loop(1, 8)
    def _(step):
        other = lax.rem(z + step, 8)
        layer_copy(other, other, 0).wait_recv()
        layer_copy(other, other, 1).wait_recv()

    line_out[0:40, :] = jnp.sum(layer_in[...], axis=0)
    line_out[40:48, :] = rows_total[0:8, 0:128]
    line_out[48:56, :] = jnp.concatenate([rows_total[0:8, 128:160], jnp.zeros((8, 96), f32)], axis=1)
    frame_other[...] = jnp.sum(frame_layer[...], axis=0)

    def line_copy(other, slot):
        return pltpu.make_async_remote_copy(
            src_ref=line_out, dst_ref=line_in.at[slot], send_sem=send_line.at[other], recv_sem=recv_line.at[slot],
            device_id=at_x(other), device_id_type=MESH,
        )

    for step in (1, 2, 3):
        line_copy(lax.rem(x + step, 4), x).start()
    line_in[x] = line_out[...]
    flip = copy(frame_other, frame_last, 12, (lax.rem(space + 16, 32), tm))
    flip.start()
    sent.append(flip)

    pairs.append(pair_stage(1))
    crosses = [cross_stage(0, pairs[0])]

    for step in (1, 2, 3):
        other = lax.rem(x + step, 4)
        line_copy(other, other).wait_recv()
    summed = jnp.sum(line_in[...], axis=0)
    for half in range(2):
        ring_out[half, 0:16, :] = summed[16 * half : 16 * half + 16]
        ring_out[half, 16:40, :] = summed[32:56]

    def ring_copy(other, slot):
        return pltpu.make_async_remote_copy(
            src_ref=ring_out.at[other // 4], dst_ref=ring_in.at[slot], send_sem=send_ring.at[other], recv_sem=recv_ring.at[slot],
            device_id=at_y(other), device_id_type=MESH,
        )

    @pl.loop(1, 8)
    def _(step):
        ring_copy(lax.rem(y + step, 8), y).start()

    ring_in[y] = ring_out[y_hi]
    crosses.append(cross_stage(1, pairs[1]))

    flip.wait_recv()
    frame_in_place = frame_other[...] + frame_last[...]
    out_frames[core] = frame_in_place
    swap_back = copy(out_frames.at[core], out_frames.at[core], 13, other_core)
    swap_back.start()
    sent.append(swap_back)

    for chunk in range(2):
        crosses[chunk].wait_recv()
        value = part[chunk, x, lax.rem(y_lo, 2), y_lo // 2] + cross_in[chunk]
        stacked = jnp.concatenate(
            [value[:, 128 * group : 128 * group + 128] for group in range(5)] + [jnp.zeros((8, 128), f32)], axis=0
        )
        turned = stacked.T
        for place in range(4):
            tiles[pl.ds(4 * chunk + place, 32, stride=8), :] = turned[32 * place : 32 * place + 32, :]

    def tile_copy(other, slot):
        return pltpu.make_async_remote_copy(
            src_ref=tiles.at[pl.ds(pl.multiple_of(other * 8, 8), 8), :],
            dst_ref=gathered.at[pl.ds(pl.multiple_of(slot * 8, 8), 8), :],
            send_sem=send_space.at[other], recv_sem=recv_space.at[slot],
            device_id=(other, tm), device_id_type=MESH,
        )

    @pl.loop(1, 32)
    def _(step):
        tile_copy(lax.rem(space + step, 32), space).start()

    own = pl.ds(pl.multiple_of(space * 8, 8), 8)
    gathered[own, :] = tiles[own, :]

    @pl.loop(1, 8)
    def _(step):
        other = lax.rem(y + step, 8)
        ring_copy(other, other).wait_recv()

    final = jnp.sum(ring_in[:, 0:24, :], axis=0)
    own_rows = jnp.sum(ring_in[pl.ds(y_hi * 4, 4), 24:40, :], axis=0)
    out_rows[:, 0:128] = own_rows[0:8]
    out_rows[:, 128:160] = own_rows[8:16, 0:32]
    out_cols[:, 0:128] = final[0:16]
    for half in range(2):
        out_cols[8 * half : 8 * half + 8, 128:160] = jnp.where(
            y_hi == 0, final[16:24, 32 * half : 32 * half + 32], final[16:24, 64 + 32 * half : 96 + 32 * half]
        )

    @pl.loop(1, 32)
    def _(step):
        other = lax.rem(space + step, 32)
        tile_copy(other, other).wait_recv()

    hi, lo = halves(gathered[...].T)
    result = dot(hi, rows_hi[...], NT) + dot(hi, rows_lo[...], NT) + dot(lo, rows_hi[...], NT)
    for group in range(5):
        for half in range(2):
            base = 24 * group
            out_core[half * 5 + group, 0:8, :] = result[base + 8 * half : base + 8 * half + 8]
            out_core[half * 5 + group, 8:12, :] = result[base + 16 + 4 * half : base + 20 + 4 * half]

    swap_back.wait_recv()
    for each in sent:
        each.wait_send()

    @pl.loop(1, 8)
    def _(step):
        other = lax.rem(z + step, 8)
        layer_copy(other, z, 0).wait_send()
        layer_copy(other, z, 1).wait_send()
        ring_copy(lax.rem(y + step, 8), y).wait_send()

    for step in (1, 2, 3):
        line_copy(lax.rem(x + step, 4), x).wait_send()

    @pl.loop(1, 32)
    def _(step):
        tile_copy(lax.rem(space + step, 32), space).wait_send()


def per_device(
    video_slab, first_cols, first_frames, second_rows, second_frames, third_rows, third_cols, core_rows, core_cols, core_frames,
):
    arguments = (
        video_slab, first_cols.T, third_cols.T, core_cols.T, first_frames.T, second_frames.T, core_frames.T,
        second_rows, third_rows, core_rows.T,
    )
    vmem = pl.BlockSpec(memory_space=pltpu.VMEM)
    dma = pltpu.SemaphoreType.DMA
    scratch = [pltpu.VMEM(each.shape, f32) for each in arguments] + [
        pltpu.VMEM((4, 320, 128), f32),
        pltpu.VMEM((576, 512), bf16), pltpu.VMEM((576, 512), bf16),
        pltpu.VMEM((384, 256), bf16), pltpu.VMEM((384, 256), bf16),
        pltpu.VMEM((320, 256), bf16), pltpu.VMEM((320, 256), bf16),
        pltpu.VMEM((512, 2048), bf16),
        pltpu.VMEM((4, 256, 256), f32),
        pltpu.VMEM((2, 5, 4, 32, 256), bf16), pltpu.VMEM((2, 5, 4, 32, 256), bf16),
        pltpu.VMEM((256, 1024), bf16), pltpu.VMEM((256, 1024), bf16),
        pltpu.VMEM((96, 1024), f32),
        pltpu.VMEM((2, 4, 2, 2, 24, 640), f32),
        pltpu.VMEM((2, 2, 2, 24, 640), f32), pltpu.VMEM((2, 2, 2, 24, 640), f32), pltpu.VMEM((2, 2, 2, 24, 640), f32),
        pltpu.VMEM((2, 2, 24, 640), f32),
        pltpu.VMEM((2, 24, 640), f32),
        pltpu.VMEM((256, 128), f32), pltpu.VMEM((256, 128), f32),
        pltpu.VMEM((2, 8, 40, 128), f32), pltpu.VMEM((8, 40, 128), f32),
        pltpu.VMEM((8, 40, 128), f32), pltpu.VMEM((8, 40, 128), f32),
        pltpu.VMEM((2, 48, 128), f32), pltpu.VMEM((48, 128), f32), pltpu.VMEM((8, 48, 128), f32),
        pltpu.VMEM((48, 128), f32), pltpu.VMEM((48, 128), f32),
        pltpu.VMEM((56, 128), f32), pltpu.VMEM((4, 56, 128), f32),
        pltpu.VMEM((2, 40, 128), f32), pltpu.VMEM((8, 40, 128), f32),
        dma((13,)), dma((14,)), dma((14,)), dma((32,)), dma((32,)), dma((2, 8)), dma((2, 8)), dma((4,)), dma((4,)), dma((8,)), dma((8,)),
    ]
    rows, cols, frames, core = pl.pallas_call(
        kernel,
        out_shape=[
            jax.ShapeDtypeStruct((8, 160), f32),
            jax.ShapeDtypeStruct((16, 160), f32),
            jax.ShapeDtypeStruct((2, 48, 128), f32),
            jax.ShapeDtypeStruct((10, 12, 320), f32),
        ],
        in_specs=[pl.BlockSpec(memory_space=pltpu.HBM)] * 10,
        out_specs=[vmem] * 4,
        scratch_shapes=scratch,
        compiler_params=pltpu.CompilerParams(collective_id=0, has_side_effects=True, vmem_limit_bytes=60 * 2**20),
    )(*arguments)
    return rows, cols, frames.reshape(96, 128).T, core.transpose(2, 0, 1)


def solution(mesh):
    return jax.shard_map(
        per_device,
        mesh=mesh,
        in_specs=(
            P("space", None, "tm"),
            P(),
            P("tm", None),
            P("space", None),
            P("tm", None),
            P("space", None),
            P(),
            P(),
            P(),
            P("tm", None),
        ),
        out_specs=(P("space", None), P("space", None), P("tm", None), P(None, "space", "tm")),
        check_vma=False,
    )
```

time: 336 us -> 69.1 us (0.21)
  the two profiles are of different devices: /device:TPU:32 before, /device:TPU:1 now
where the time goes in v1:
time: 69.1 us; the launch traced here: 68.8 us
  Pallas kernels  62.4 us (90%)
  local copies, waits for them, and re-layouts  5.69 us (8%)
    pallas_call x1, Pallas kernels, per_device(): pl.pallas_call(kernel, out_shape=[jax.ShapeDtypeStruct((8, 160), f32), ja...  62.4 us
    unnamed x4, local copies, waits for them, and re-layouts  5.69 us

profile of v1, /device:TPU:1, one launch (start us, length us, event | category | flops | bytes accessed | tf_op | source)
XLA Modules:
  0.0 68.8 jit_solution(16550758475557671339)
XLA Ops:
  0.6 62.4 %shard_map.129 = (f32[8,160]{1,0:T(8,128)}, f32[16,160]{1,0:T(8,128)}, f32[2,48,128]{2,1,0:T(8,128)}, f32[10,12,320]{2,1,0:T(8,128)}) custom-call(f32[8,512,128]{2,1,0:T(8,128)} %slab_given.1, f32[160,512]{1,0:T(8,128)} %bitcast.12, f32[96,512]{1,0:T(8,128)} %bitcast.15, f32[320,512]{1,0:T(8,128)} %bitcast.11, f32[160,128]{1,0:T(8,128)} %bitcast.17, ...), custom_call_target="tpu_custom_call" | custom-call | tf_op jit(solution)/shard_map/pallas_call | solution.py:473
  63.1 1.3 %copy.18 = f32[8,160]{1,0:T(8,128)} copy(f32[8,160]{1,0:T(8,128)} %get-tuple-element.16) | data formatting | bytes 10240
  64.4 1.3 %copy.19 = f32[16,160]{1,0:T(8,128)} copy(f32[16,160]{1,0:T(8,128)} %get-tuple-element.17) | data formatting | bytes 20480
  65.7 1.4 %copy.20 = f32[128,96]{0,1:T(8,128)} copy(f32[128,96]{0,1:T(8,128)} %bitcast.19) | data formatting | bytes 98304
  67.1 1.7 %copy.21 = f32[320,10,12]{0,2,1:T(8,128)} copy(f32[320,10,12]{0,2,1:T(8,128)} %bitcast.14) | data formatting | bytes 307200

commit v2 on v1

v2 whole, which is shorter than its diff:
```python
import functools

import jax
import jax.numpy as jnp
from jax import lax
from jax.experimental import pallas as pl
from jax.experimental.pallas import tpu as pltpu
from jax.sharding import PartitionSpec as P

MESH = pl.DeviceIdType.MESH
f32, bf16 = jnp.float32, jnp.bfloat16

NN = (((1,), (0,)), ((), ()))
NT = (((1,), (1,)), ((), ()))
TN = (((0,), (0,)), ((), ()))


def dot(a, b, dims=NN):
    return lax.dot_general(a, b, dims, preferred_element_type=f32)


def halves(a):
    high = a.astype(bf16)
    return high, (a - high.astype(f32)).astype(bf16)


def kernel(
    slab_given, first_cols_given, third_cols_given, core_cols_given, first_frames_given, second_frames_given,
    core_frames_given, second_rows_given, third_rows_given,
    gathered, out_small, out_frames,
    slab, first_cols, third_cols, core_cols, first_frames, second_frames, core_frames, second_rows, third_rows,
    order, cols_hi, cols_lo, frames_hi, frames_lo, split, inner, rest_hi, rest_lo, second_hi, second_lo, third_wide,
    part, far, near, after, line, tiles,
    small, core_in, layer_out, layer_in, frame_part, frame_in, frame_layer, frame_other, frame_last,
    line_out, line_in, ring_out, ring_in,
    load_sem, send_sem, recv_sem, send_space, recv_space, send_layer, recv_layer, send_line, recv_line, send_ring, recv_ring, send_y, recv_y,
):
    space, tm = lax.axis_index("space"), lax.axis_index("tm")
    y_hi, z, core = space // 16, lax.rem(space // 2, 8), lax.rem(space, 2)
    y_lo, x = tm // 4, lax.rem(tm, 4)
    y = y_hi * 4 + y_lo

    def at_x(other):
        return (space, y_lo * 4 + other)

    def at_y(other):
        return (lax.rem(other // 4, 2) * 16 + z * 2 + core, lax.rem(other, 4) * 4 + x)

    def at_z(other):
        return (y_hi * 16 + other * 2 + core, tm)

    def load(number, source, target):
        return pltpu.make_async_copy(source, target, load_sem.at[number])

    def load_pair(pair):
        rows = pl.ds(2 * pair, 2)
        return load(pair, slab_given.at[rows], slab.at[rows])

    loads = {
        "core_cols": load(4, core_cols_given, core_cols),
        "first_cols": load(5, first_cols_given, first_cols),
        "third_cols": load(6, third_cols_given, third_cols),
        "core_frames": load(7, core_frames_given, core_frames),
        "second_rows": load(8, second_rows_given, second_rows),
        "third_rows": load(9, third_rows_given, third_rows),
        "second_frames": load(10, second_frames_given, second_frames),
        "first_frames": load(11, first_frames_given, first_frames),
    }
    for each in ("core_cols", "core_frames", "first_cols", "third_cols"):
        loads[each].start()
    for pair in range(4):
        load_pair(pair).start()
    for each in ("second_rows", "third_rows", "second_frames", "first_frames"):
        loads[each].start()

    barrier = pltpu.get_barrier_semaphore()

    def greet(device):
        pl.semaphore_signal(barrier, inc=1, device_id=device, device_id_type=MESH)

    @pl.loop(1, 16)
    def _(step):
        greet((y_hi * 16 + lax.rem(space + step, 16), tm))

    @pl.loop(1, 8)
    def _(step):
        greet(at_y(lax.rem(y + step, 8)))

    for step in (1, 2, 3):
        greet(at_x(lax.rem(x + step, 4)))

    loads["core_cols"].wait()
    loads["first_cols"].wait()
    loads["third_cols"].wait()
    loads["core_frames"].wait()
    hi, lo = halves(first_cols[...])
    cols_hi[0:160, :], cols_lo[0:160, :] = hi, lo
    hi, lo = halves(third_cols[...])
    cols_hi[160:256, :], cols_lo[160:256, :] = hi, lo
    for quarter in range(4):
        lanes = slice(128 * quarter, 128 * quarter + 128)
        order[quarter] = core_cols[:, lanes]
        for half in range(2):
            for place in range(10):
                hi, lo = halves(order[quarter, pl.ds(160 * half + place, 16, stride=10), :])
                base = 256 + 128 * half + 16 * place if place < 8 else 512 + 32 * half + 16 * (place - 8)
                cols_hi[base : base + 16, lanes], cols_lo[base : base + 16, lanes] = hi, lo

    for other in range(4):
        for place in range(4):
            base = 12 * (place * 4 + other)
            row = 24 * (other * 4 + place)
            eight = core_frames[base : base + 8, :]
            four = core_frames[base + 8 : base + 12, :]
            blank = jnp.zeros((8, 128), f32)
            blank4 = jnp.zeros((4, 128), f32)
            block = jnp.concatenate(
                [
                    jnp.concatenate([eight, blank], axis=1),
                    jnp.concatenate([blank, eight], axis=1),
                    jnp.concatenate([four, blank4], axis=1),
                    jnp.concatenate([blank4, four], axis=1),
                ],
                axis=0,
            )
            hi, lo = halves(block)
            frames_hi[row : row + 24, :], frames_lo[row : row + 24, :] = hi, lo

    def columns(pair):
        load_pair(pair).wait()
        lanes = pl.ds(pl.multiple_of(pair * 256, 256), 256)
        low_lanes = pl.ds(pl.multiple_of(pair * 256 + 1024, 256), 256)
        block = jnp.concatenate([slab[2 * pair], slab[2 * pair + 1]], axis=1)
        hi, lo = halves(block)
        split[:, lanes] = hi
        split[:, low_lanes] = lo
        product = dot(cols_hi[...], hi) + dot(cols_hi[...], lo) + dot(cols_lo[...], hi)
        inner[pair] = product[0:256, :]
        hi, lo = halves(product[512:576, :].reshape(2, 32, 256))
        rest_hi[:, pair], rest_lo[:, pair] = hi, lo
        frames(pair, *halves(product[256:512, :]))

    def frames(unit, right_hi, right_lo):
        product = (
            dot(frames_hi[...], right_hi, NT) + dot(frames_hi[...], right_lo, NT) + dot(frames_lo[...], right_hi, NT)
        )
        for half in range(2):
            part[unit, :, half] = product[:, 128 * half : 128 * half + 128].reshape(4, 4, 24, 128)

    def copy(source, target, number, device):
        return pltpu.make_async_remote_copy(
            src_ref=source, dst_ref=target, send_sem=send_sem.at[number], recv_sem=recv_sem.at[number],
            device_id=device, device_id_type=MESH,
        )

    right, left, across = lax.rem(x + 1, 4), lax.rem(x + 3, 4), lax.rem(x + 2, 4)

    sent = []

    ways = ((right, left), (left, right), (right, left), (left, right), (right, left))

    def far_copy(unit):
        return copy(part.at[unit, across], far.at[unit], 3 * unit, at_x(ways[unit][0] if unit < 4 else across))

    def near_copy(unit):
        return copy(part.at[unit, ways[unit][1]], near.at[unit], 3 * unit + 1, at_x(ways[unit][1]))

    def after_copy(unit):
        onward = ways[unit][0]
        return copy(part.at[unit, onward], after.at[unit], 3 * unit + 2, at_x(onward))

    def begin(each):
        each.start()
        sent.append(each)

    def relay(unit):
        far_copy(unit).wait_recv()
        part[unit, ways[unit][0]] += far[unit]
        begin(after_copy(unit))

    def y_copy(unit, other, slot):
        return pltpu.make_async_remote_copy(
            src_ref=part.at[unit, x, other // 4, lax.rem(other, 4)], dst_ref=line.at[unit, slot],
            send_sem=send_y.at[unit, other], recv_sem=recv_y.at[unit, slot],
            device_id=at_y(other), device_id_type=MESH,
        )

    def y_begin(unit):
        near_copy(unit).wait_recv()
        after_copy(unit).wait_recv()
        total = part[unit, x] + near[unit] + after[unit]
        if unit == 4:
            far_copy(unit).wait_recv()
            total = total + far[unit]
        part[unit, x] = total

        for step in (4, 3, 5, 2, 6, 1, 7):
            y_copy(unit, lax.rem(y + step, 8), y).start()

        line[unit, y] = part[unit, x, y_hi, y_lo]

    row = lax.rem(lax.broadcasted_iota(jnp.int32, (48, 256), 0), 24)
    lane = lax.broadcasted_iota(jnp.int32, (48, 256), 1)
    side, lane = lane // 128, lax.rem(lane, 128)
    rank = lax.rem(lane, 12)
    wanted = jnp.where(rank < 8, 8 * side + rank, 8 + 4 * side + rank)
    pick = ((row == wanted) & (lane < 120)).astype(f32).astype(bf16)
    lane_place = lax.broadcasted_iota(jnp.int32, (16, 256), 1)
    lane_place = lax.rem(lane_place, 128) // 12

    def y_end(unit):
        @pl.loop(1, 8)
        def _(step):
            other = lax.rem(y + step, 8)
            y_copy(unit, other, other).wait_recv()

        value = jnp.concatenate([jnp.sum(line[unit, 0:4], axis=0), jnp.sum(line[unit, 4:8], axis=0)], axis=1)
        turned = dot(jnp.concatenate(halves(value), axis=0), pick, TN)
        return turned.reshape(2, 8, 16, 256)

    def tile_rows(half, row):
        return pl.ds(8 * half + row, 16, stride=16)

    def unit_end(unit):
        turned = y_end(unit)
        for half in range(2):
            total = jnp.zeros((16, 256), f32)
            for place in range(8):
                total = jnp.where(lane_place == place, turned[half, place], total)
            for row in range(2):
                tiles[tile_rows(half, 2 * unit + row), :] = total[:, 128 * row : 128 * row + 128]

    def rest_end():
        turned = y_end(4)
        for half in range(2):
            for pair in range(4):
                total = jnp.where(lane_place == 8, turned[half, 2 * pair], turned[half, 2 * pair + 1])
                for row in range(2):
                    rows = tile_rows(half, 2 * pair + row)
                    lanes = slice(128 * row, 128 * row + 128)
                    tiles[rows, :] = jnp.where(lane_place[:, lanes] < 8, tiles[rows, :], total[:, lanes])

    columns(0)
    pl.semaphore_wait(barrier, 25)
    begin(far_copy(0))
    begin(near_copy(0))
    columns(1)
    begin(far_copy(1))
    begin(near_copy(1))
    columns(2)
    begin(near_copy(2))
    columns(3)
    frames(4, rest_hi[...].reshape(256, 256), rest_lo[...].reshape(256, 256))

    index_k = lax.broadcasted_iota(jnp.int32, (8, 1024), 0)
    index_l = lax.broadcasted_iota(jnp.int32, (8, 1024), 1) // 128
    spread = (index_k == index_l).astype(f32)

    for each in ("second_rows", "third_rows", "second_frames", "first_frames"):
        loads[each].wait()

    def widen(values):
        return lax.dot_general(values, spread, TN, precision=lax.Precision.HIGHEST, preferred_element_type=f32)

    wide_second = widen(second_rows[...])
    for row in range(8):
        lanes = slice(row * 128, row * 128 + 128)
        value = second_frames[...] * wide_second[:, lanes]
        hi, lo = halves(value)
        second_hi[0:128, lanes], second_lo[0:128, lanes] = hi[0:128], lo[0:128]
        for copies in range(4):
            rows = slice(128 + 32 * copies, 160 + 32 * copies)
            second_hi[rows, lanes], second_lo[rows, lanes] = hi[128:160], lo[128:160]
    third_wide[...] = widen(third_rows[...])

    second = (
        dot(split[:, 0:1024], second_hi[...], NT)
        + dot(split[:, 1024:2048], second_hi[...], NT)
        + dot(split[:, 0:1024], second_lo[...], NT)
    )
    main = second[:, 0:128].reshape(2, 8, 2, 16, 128)
    tail = second[:, 128:256].reshape(2, 8, 2, 2, 8, 128)
    quarter = lax.broadcasted_iota(jnp.int32, (8, 8, 128), 2) // 32
    for which in range(2):
        small[which, :, 0:16, :] = main[0, :, which]
        small[which, :, 16:32, :] = main[1, :, which]
        small[which, :, 32:40, :] = jnp.where(
            quarter < 2,
            jnp.where(quarter == 0, tail[0, :, which, 0], tail[0, :, which, 1]),
            jnp.where(quarter == 2, tail[1, :, which, 0], tail[1, :, which, 1]),
        )

    total = jnp.zeros((96, 128), f32)
    for row in range(8):
        place = slice((row % 2) * 128, (row % 2) * 128 + 128)
        total = total + inner[row // 2, 160:256, place] * third_wide[:, row * 128 : row * 128 + 128]
    frame_part[...] = total.reshape(2, 48, 128)

    other_core = (y_hi * 16 + z * 2 + 1 - core, tm)
    swap = copy(small.at[1 - core], core_in, 15, other_core)
    swap.start()
    swap_frames = copy(frame_part.at[1 - core], frame_in, 16, other_core)
    swap_frames.start()
    sent.extend([swap, swap_frames])

    relay(0)
    begin(far_copy(2))
    relay(1)
    begin(far_copy(3))

    rows_total = jnp.zeros((16, 160), f32)
    index_k = lax.broadcasted_iota(jnp.int32, (16, 256), 0)
    index_l = lax.broadcasted_iota(jnp.int32, (16, 256), 1) // 128
    for pair in range(4):
        value = inner[pair, 0:160, :] * jnp.concatenate([first_frames[...], first_frames[...]], axis=1)
        hi, lo = halves(value)
        ones = (index_k == index_l + 2 * pair).astype(f32).astype(bf16)
        rows_total = rows_total + dot(ones, hi, NT) + dot(ones, lo, NT)

    begin(near_copy(3))

    swap.wait_recv()
    layer_out[...] = small[core] + core_in[...]
    swap_frames.wait_recv()
    frame_layer[z] = frame_part[core] + frame_in[...]

    def layer_copy(other, slot, kind):
        if kind == 0:
            source, target = layer_out.at[other], layer_in.at[slot]
        else:
            source, target = frame_layer.at[z], frame_layer.at[slot]
        return pltpu.make_async_remote_copy(
            src_ref=source, dst_ref=target, send_sem=send_layer.at[kind, other], recv_sem=recv_layer.at[kind, slot],
            device_id=at_z(other), device_id_type=MESH,
        )

    @pl.loop(1, 8)
    def _(step):
        other = lax.rem(z + step, 8)
        layer_copy(other, z, 0).start()
        layer_copy(other, z, 1).start()

    layer_in[z] = layer_out[z]

    y_begin(0)
    relay(2)
    begin(near_copy(4))
    begin(after_copy(4))
    y_begin(1)
    relay(3)
    begin(far_copy(4))
    y_begin(2)

    @pl.loop(1, 8)
    def _(step):
        other = lax.rem(z + step, 8)
        layer_copy(other, other, 0).wait_recv()
        layer_copy(other, other, 1).wait_recv()

    line_out[0:40, :] = jnp.sum(layer_in[...], axis=0)
    line_out[40:48, :] = rows_total[0:8, 0:128]
    line_out[48:56, :] = jnp.concatenate([rows_total[0:8, 128:160], jnp.zeros((8, 96), f32)], axis=1)
    frame_other[...] = jnp.sum(frame_layer[...], axis=0)

    def line_copy(other, slot):
        return pltpu.make_async_remote_copy(
            src_ref=line_out, dst_ref=line_in.at[slot], send_sem=send_line.at[other], recv_sem=recv_line.at[slot],
            device_id=at_x(other), device_id_type=MESH,
        )

    for step in (1, 2, 3):
        line_copy(lax.rem(x + step, 4), x).start()
    line_in[x] = line_out[...]
    flip = copy(frame_other, frame_last, 17, (lax.rem(space + 16, 32), tm))
    flip.start()
    sent.append(flip)

    y_begin(3)
    unit_end(0)
    y_begin(4)
    unit_end(1)

    for step in (1, 2, 3):
        other = lax.rem(x + step, 4)
        line_copy(other, other).wait_recv()
    summed = jnp.sum(line_in[...], axis=0)
    for half in range(2):
        ring_out[half, 0:16, :] = summed[16 * half : 16 * half + 16]
        ring_out[half, 16:40, :] = summed[32:56]

    def ring_copy(other, slot):
        return pltpu.make_async_remote_copy(
            src_ref=ring_out.at[other // 4], dst_ref=ring_in.at[slot], send_sem=send_ring.at[other], recv_sem=recv_ring.at[slot],
            device_id=at_y(other), device_id_type=MESH,
        )

    @pl.loop(1, 8)
    def _(step):
        ring_copy(lax.rem(y + step, 8), y).start()

    ring_in[y] = ring_out[y_hi]

    flip.wait_recv()
    frame_in_place = frame_other[...] + frame_last[...]
    out_frames[core] = frame_in_place
    swap_back = copy(out_frames.at[core], out_frames.at[core], 18, other_core)
    swap_back.start()
    sent.append(swap_back)

    unit_end(2)
    unit_end(3)
    rest_end()

    mine = lax.rem(space, 16)
    tile_view = tiles.reshape(16, 2, 8, 128)

    def tile_copy(other, slot):
        return pltpu.make_async_remote_copy(
            src_ref=tile_view.at[other], dst_ref=gathered.at[:, slot],
            send_sem=send_space.at[other], recv_sem=recv_space.at[slot],
            device_id=(y_hi * 16 + other, tm), device_id_type=MESH,
        )

    for step in (8, 7, 9, 6, 10, 5, 11, 4, 12, 3, 13, 2, 14, 1, 15):
        tile_copy(lax.rem(mine + step, 16), mine).start()

    gathered[:, mine] = tile_view[mine]

    @pl.loop(1, 8)
    def _(step):
        other = lax.rem(y + step, 8)
        ring_copy(other, other).wait_recv()

    final = jnp.sum(ring_in[:, 0:24, :], axis=0)
    out_small[0:24, :] = final
    out_small[24:40, :] = jnp.sum(ring_in[pl.ds(y_hi * 4, 4), 24:40, :], axis=0)

    @pl.when(y_hi == 0)
    def _():
        out_small[16:24, 0:64] = final[16:24, 0:64]

    @pl.when(y_hi == 1)
    def _():
        out_small[16:24, 0:64] = final[16:24, 64:128]

    for each in sent:
        each.wait_send()

    @pl.loop(1, 8)
    def _(step):
        other = lax.rem(z + step, 8)
        layer_copy(other, z, 0).wait_send()
        layer_copy(other, z, 1).wait_send()
        other = lax.rem(y + step, 8)
        ring_copy(other, y).wait_send()
        for unit in range(5):
            y_copy(unit, other, y).wait_send()

    for step in (1, 2, 3):
        line_copy(lax.rem(x + step, 4), x).wait_send()

    @pl.loop(1, 16)
    def _(step):
        tile_copy(lax.rem(mine + step, 16), mine).wait_send()

    @pl.loop(1, 16)
    def _(step):
        other = lax.rem(mine + step, 16)
        tile_copy(other, other).wait_recv()

    swap_back.wait_recv()


def finish(gathered, small, frames, core_rows, out_rows, out_cols, out_frames, out_core):
    out_rows[:, 0:128] = small[24:32, :]
    out_rows[:, 128:160] = small[32:40, 0:32]
    out_cols[:, 0:128] = small[0:16, :]
    for half in range(2):
        out_cols[8 * half : 8 * half + 8, 128:160] = small[16:24, 32 * half : 32 * half + 32]
    out_frames[...] = frames[...]
    hi, lo = halves(gathered[...].reshape(256, 128).T)
    rows_hi, rows_lo = halves(core_rows[...])
    result = dot(hi, rows_hi, NT) + dot(hi, rows_lo, NT) + dot(lo, rows_hi, NT)
    for place in range(10):
        out_core[place] = result[12 * place : 12 * place + 12]


def per_device(
    video_slab, first_cols, first_frames, second_rows, second_frames, third_rows, third_cols, core_rows, core_cols, core_frames,
):
    arguments = (
        video_slab, first_cols.T, third_cols.T, core_cols.T, first_frames.T, second_frames.T, core_frames.T,
        second_rows, third_rows,
    )
    vmem = pl.BlockSpec(memory_space=pltpu.VMEM)
    dma = pltpu.SemaphoreType.DMA
    scratch = [pltpu.VMEM(each.shape, f32) for each in arguments] + [
        pltpu.VMEM((4, 320, 128), f32),
        pltpu.VMEM((576, 512), bf16), pltpu.VMEM((576, 512), bf16),
        pltpu.VMEM((384, 256), bf16), pltpu.VMEM((384, 256), bf16),
        pltpu.VMEM((512, 2048), bf16),
        pltpu.VMEM((4, 256, 256), f32),
        pltpu.VMEM((2, 4, 32, 256), bf16), pltpu.VMEM((2, 4, 32, 256), bf16),
        pltpu.VMEM((256, 1024), bf16), pltpu.VMEM((256, 1024), bf16),
        pltpu.VMEM((96, 1024), f32),
        pltpu.VMEM((5, 4, 2, 4, 24, 128), f32), *[pltpu.VMEM((5, 2, 4, 24, 128), f32)] * 3,
        pltpu.VMEM((5, 8, 24, 128), f32),
        pltpu.VMEM((256, 128), f32),
        pltpu.VMEM((2, 8, 40, 128), f32), pltpu.VMEM((8, 40, 128), f32),
        pltpu.VMEM((8, 40, 128), f32), pltpu.VMEM((8, 40, 128), f32),
        pltpu.VMEM((2, 48, 128), f32), pltpu.VMEM((48, 128), f32), pltpu.VMEM((8, 48, 128), f32),
        pltpu.VMEM((48, 128), f32), pltpu.VMEM((48, 128), f32),
        pltpu.VMEM((56, 128), f32), pltpu.VMEM((4, 56, 128), f32),
        pltpu.VMEM((2, 40, 128), f32), pltpu.VMEM((8, 40, 128), f32),
        dma((12,)), dma((20,)), dma((20,)), dma((16,)), dma((16,)), dma((2, 8)), dma((2, 8)), dma((4,)), dma((4,)), dma((8,)), dma((8,)), dma((5, 8)), dma((5, 8)),
    ]
    gathered, small, frames = pl.pallas_call(
        kernel,
        out_shape=[
            jax.ShapeDtypeStruct((2, 16, 8, 128), f32),
            jax.ShapeDtypeStruct((40, 128), f32),
            jax.ShapeDtypeStruct((2, 48, 128), f32),
        ],
        in_specs=[pl.BlockSpec(memory_space=pltpu.HBM)] * 9,
        out_specs=[vmem] * 3,
        scratch_shapes=scratch,
        compiler_params=pltpu.CompilerParams(collective_id=0, has_side_effects=True, vmem_limit_bytes=60 * 2**20),
    )(*arguments)
    rows, cols, frames, core = pl.pallas_call(
        finish,
        out_shape=[
            jax.ShapeDtypeStruct((8, 160), f32),
            jax.ShapeDtypeStruct((16, 160), f32),
            jax.ShapeDtypeStruct((2, 48, 128), f32),
            jax.ShapeDtypeStruct((10, 12, 320), f32),
        ],
        in_specs=[vmem] * 4,
        out_specs=[vmem] * 4,
        compiler_params=pltpu.CompilerParams(vmem_limit_bytes=60 * 2**20),
    )(gathered, small, frames, core_rows.T)
    return rows, cols, frames.reshape(96, 128).T, core.transpose(2, 0, 1)


def solution(mesh):
    return jax.shard_map(
        per_device,
        mesh=mesh,
        in_specs=(
            P("space", None, "tm"),
            P(),
            P("tm", None),
            P("space", None),
            P("tm", None),
            P("space", None),
            P(),
            P(),
            P(),
            P("tm", None),
        ),
        out_specs=(P("space", None), P("space", None), P("tm", None), P(None, "space", "tm")),
        check_vma=False,
    )
```

time: 69.1 us -> 54.8 us (0.79)
  Pallas kernels: 62.4 us -> 54.1 us
  local copies, waits for them, and re-layouts: 5.69 us -> 0 us
    pallas_call x1 -> x2, Pallas kernels: 62.4 us -> 54.1 us  [the longest x1 51.9 us: per_device(): pl.pallas_call(kernel, out_shape=[jax.ShapeDtypeStruct((2, 16, 8, 128), f...]
    unnamed x4 -> x0, local copies, waits for them, and re-layouts: 5.69 us -> none
where the time goes in v2:
time: 54.8 us; the launch traced here: 54.7 us
  Pallas kernels  54.1 us (99%)
  between operations  0.64 us (1%)
    pallas_call x1, Pallas kernels, per_device(): pl.pallas_call(kernel, out_shape=[jax.ShapeDtypeStruct((2, 16, 8, 128), f...  51.9 us
    pallas_call x1, Pallas kernels, per_device(): pl.pallas_call(finish, out_shape=[jax.ShapeDtypeStruct((8, 160), f32), ja...  2.16 us

profile of v2, /device:TPU:1, one launch (start us, length us, event | category | flops | bytes accessed | tf_op | source)
XLA Modules:
  0.0 54.7 jit_solution(5459574921625218016)
XLA Ops:
  0.6 51.9 %shard_map.129 = (f32[2,16,8,128]{3,2,1,0:T(8,128)}, f32[40,128]{1,0:T(8,128)}, f32[2,48,128]{2,1,0:T(8,128)}) custom-call(f32[8,512,128]{2,1,0:T(8,128)} %slab_given.1, f32[160,512]{1,0:T(8,128)} %bitcast.13, f32[96,512]{1,0:T(8,128)} %bitcast.14, f32[320,512]{1,0:T(8,128)} %bitcast.11, f32[160,128]{1,0:T(8,128)} %bitcast.16, f32[160,128]{1,0:T(8,128)} %bitcast.17, ...), custom_call_target="tpu_custom_call" | custom-call | tf_op jit(solution)/shard_map/pallas_call | solution.py:517
  52.5 2.2 %shard_map.130 = (f32[8,160]{1,0:T(8,128)}, f32[16,160]{1,0:T(8,128)}, f32[2,48,128]{2,1,0:T(8,128)}, f32[10,12,320]{2,1,0:T(8,128)}) custom-call(f32[2,16,8,128]{3,2,1,0:T(8,128)} %get-tuple-element.11.gathered, f32[40,128]{1,0:T(8,128)} %get-tuple-element.12.small, f32[2,48,128]{2,1,0:T(8,128)} %get-tuple-element.13.frames, f32[320,256]{1,0:T(8,128)} %bitcast.12), custom_call_target="tpu_custom_call" | custom-call | tf_op jit(solution)/shard_map/pallas_call | solution.py:529

commit v3 on v2

--- a/solution.py
+++ b/solution.py
@@ -31,9 +31,10 @@
     slab, first_cols, third_cols, core_cols, first_frames, second_frames, core_frames, second_rows, third_rows,
     order, cols_hi, cols_lo, frames_hi, frames_lo, split, inner, rest_hi, rest_lo, second_hi, second_lo, third_wide,
     part, far, near, after, line, tiles,
-    small, core_in, layer_out, layer_in, frame_part, frame_in, frame_layer, frame_other, frame_last,
-    line_out, line_in, ring_out, ring_in,
+    small, core_in, layer_out, layer_in, frame_part, frame_in, frame_pair, frame_other, frame_layer,
+    line_out, line_in, ring_in, piece_in,
     load_sem, send_sem, recv_sem, send_space, recv_space, send_layer, recv_layer, send_line, recv_line, send_ring, recv_ring, send_y, recv_y,
+    send_piece, recv_piece, send_quarter, recv_quarter,
 ):
     space, tm = lax.axis_index("space"), lax.axis_index("tm")
     y_hi, z, core = space // 16, lax.rem(space // 2, 8), lax.rem(space, 2)
@@ -66,11 +67,12 @@
         "second_frames": load(10, second_frames_given, second_frames),
         "first_frames": load(11, first_frames_given, first_frames),
     }
-    for each in ("core_cols", "core_frames", "first_cols", "third_cols"):
-        loads[each].start()
-    for pair in range(4):
+    loads["core_cols"].start()
+    load_pair(0).start()
+    loads["core_frames"].start()
+    for pair in (1, 2, 3):
         load_pair(pair).start()
-    for each in ("second_rows", "third_rows", "second_frames", "first_frames"):
+    for each in ("first_cols", "third_cols", "second_rows", "third_rows", "second_frames", "first_frames"):
         loads[each].start()
 
     barrier = pltpu.get_barrier_semaphore()
@@ -86,17 +88,12 @@
     def _(step):
         greet(at_y(lax.rem(y + step, 8)))
 
+    greet(((1 - y_hi) * 16 + z * 2 + 1 - core, tm))
     for step in (1, 2, 3):
         greet(at_x(lax.rem(x + step, 4)))
 
     loads["core_cols"].wait()
-    loads["first_cols"].wait()
-    loads["third_cols"].wait()
-    loads["core_frames"].wait()
-    hi, lo = halves(first_cols[...])
-    cols_hi[0:160, :], cols_lo[0:160, :] = hi, lo
-    hi, lo = halves(third_cols[...])
-    cols_hi[160:256, :], cols_lo[160:256, :] = hi, lo
+
     for quarter in range(4):
         lanes = slice(128 * quarter, 128 * quarter + 128)
         order[quarter] = core_cols[:, lanes]
@@ -105,6 +102,8 @@
                 hi, lo = halves(order[quarter, pl.ds(160 * half + place, 16, stride=10), :])
                 base = 256 + 128 * half + 16 * place if place < 8 else 512 + 32 * half + 16 * (place - 8)
                 cols_hi[base : base + 16, lanes], cols_lo[base : base + 16, lanes] = hi, lo
+
+    loads["core_frames"].wait()
 
     for other in range(4):
         for place in range(4):
@@ -128,17 +127,19 @@
 
     def columns(pair):
         load_pair(pair).wait()
-        lanes = pl.ds(pl.multiple_of(pair * 256, 256), 256)
-        low_lanes = pl.ds(pl.multiple_of(pair * 256 + 1024, 256), 256)
         block = jnp.concatenate([slab[2 * pair], slab[2 * pair + 1]], axis=1)
         hi, lo = halves(block)
-        split[:, lanes] = hi
-        split[:, low_lanes] = lo
-        product = dot(cols_hi[...], hi) + dot(cols_hi[...], lo) + dot(cols_lo[...], hi)
-        inner[pair] = product[0:256, :]
-        hi, lo = halves(product[512:576, :].reshape(2, 32, 256))
+        split[:, pair * 256 : pair * 256 + 256] = hi
+        split[:, pair * 256 + 1024 : pair * 256 + 1280] = lo
+        product = dot(cols_hi[256:576], hi) + dot(cols_hi[256:576], lo) + dot(cols_lo[256:576], hi)
+        hi, lo = halves(product[256:320, :].reshape(2, 32, 256))
         rest_hi[:, pair], rest_lo[:, pair] = hi, lo
-        frames(pair, *halves(product[256:512, :]))
+        frames(pair, *halves(product[0:256, :]))
+
+    def other_columns(pair):
+        hi = split[:, pair * 256 : pair * 256 + 256]
+        lo = split[:, pair * 256 + 1024 : pair * 256 + 1280]
+        inner[pair] = dot(cols_hi[0:256], hi) + dot(cols_hi[0:256], lo) + dot(cols_lo[0:256], hi)
 
     def frames(unit, right_hi, right_lo):
         product = (
@@ -157,26 +158,36 @@
 
     sent = []
 
-    ways = ((right, left), (left, right), (right, left), (left, right), (right, left))
-
-    def far_copy(unit):
-        return copy(part.at[unit, across], far.at[unit], 3 * unit, at_x(ways[unit][0] if unit < 4 else across))
-
-    def near_copy(unit):
-        return copy(part.at[unit, ways[unit][1]], near.at[unit], 3 * unit + 1, at_x(ways[unit][1]))
-
-    def after_copy(unit):
-        onward = ways[unit][0]
-        return copy(part.at[unit, onward], after.at[unit], 3 * unit + 2, at_x(onward))
+    ways = ((right, left), (left, right), (right, left), (left, right), (right, left), (left, right))
+
+    def own(piece, owner):
+        return part.at[piece, owner] if piece < 4 else part.at[4, owner, piece - 4]
+
+    def landing(ref, piece):
+        return ref.at[piece] if piece < 4 else ref.at[4, piece - 4]
+
+    def far_copy(piece):
+        return copy(own(piece, across), landing(far, piece), 3 * piece, at_x(ways[piece][0]))
+
+    def near_copy(piece):
+        back = ways[piece][1]
+        return copy(own(piece, back), landing(near, piece), 3 * piece + 1, at_x(back))
+
+    def after_copy(piece):
+        onward = ways[piece][0]
+        return copy(own(piece, onward), landing(after, piece), 3 * piece + 2, at_x(onward))
 
     def begin(each):
         each.start()
         sent.append(each)
 
-    def relay(unit):
-        far_copy(unit).wait_recv()
-        part[unit, ways[unit][0]] += far[unit]
-        begin(after_copy(unit))
+    def relay(piece):
+        far_copy(piece).wait_recv()
+        if piece < 4:
+            part[piece, ways[piece][0]] += far[piece]
+        else:
+            part[4, ways[piece][0], piece - 4] += far[4, piece - 4]
+        begin(after_copy(piece))
 
     def y_copy(unit, other, slot):
         return pltpu.make_async_remote_copy(
@@ -186,13 +197,10 @@
         )
 
     def y_begin(unit):
-        near_copy(unit).wait_recv()
-        after_copy(unit).wait_recv()
-        total = part[unit, x] + near[unit] + after[unit]
-        if unit == 4:
-            far_copy(unit).wait_recv()
-            total = total + far[unit]
-        part[unit, x] = total
+        for piece in (unit,) if unit < 4 else (4, 5):
+            near_copy(piece).wait_recv()
+            after_copy(piece).wait_recv()
+        part[unit, x] = part[unit, x] + near[unit] + after[unit]
 
         for step in (4, 3, 5, 2, 6, 1, 7):
             y_copy(unit, lax.rem(y + step, 8), y).start()
@@ -241,16 +249,30 @@
                     tiles[rows, :] = jnp.where(lane_place[:, lanes] < 8, tiles[rows, :], total[:, lanes])
 
     columns(0)
-    pl.semaphore_wait(barrier, 25)
+    pl.semaphore_wait(barrier, 26)
     begin(far_copy(0))
     begin(near_copy(0))
     columns(1)
     begin(far_copy(1))
     begin(near_copy(1))
     columns(2)
+    begin(far_copy(2))
+    columns(3)
+    begin(far_copy(3))
+    frames(4, rest_hi[...].reshape(256, 256), rest_lo[...].reshape(256, 256))
+
+    loads["first_cols"].wait()
+    loads["third_cols"].wait()
+    hi, lo = halves(first_cols[...])
+    cols_hi[0:160, :], cols_lo[0:160, :] = hi, lo
+    hi, lo = halves(third_cols[...])
+    cols_hi[160:256, :], cols_lo[160:256, :] = hi, lo
+    for pair in range(4):
+        other_columns(pair)
+
+    relay(0)
+    begin(far_copy(4))
     begin(near_copy(2))
-    columns(3)
-    frames(4, rest_hi[...].reshape(256, 256), rest_lo[...].reshape(256, 256))
 
     index_k = lax.broadcasted_iota(jnp.int32, (8, 1024), 0)
     index_l = lax.broadcasted_iota(jnp.int32, (8, 1024), 1) // 128
@@ -290,23 +312,50 @@
             jnp.where(quarter == 2, tail[1, :, which, 0], tail[1, :, which, 1]),
         )
 
+    relay(1)
+    begin(far_copy(5))
+
     total = jnp.zeros((96, 128), f32)
     for row in range(8):
         place = slice((row % 2) * 128, (row % 2) * 128 + 128)
         total = total + inner[row // 2, 160:256, place] * third_wide[:, row * 128 : row * 128 + 128]
-    frame_part[...] = total.reshape(2, 48, 128)
+    frame_part[...] = total.reshape(2, 2, 24, 128)
 
     other_core = (y_hi * 16 + z * 2 + 1 - core, tm)
-    swap = copy(small.at[1 - core], core_in, 15, other_core)
+    swap = copy(small.at[1 - core], core_in, 18, other_core)
     swap.start()
-    swap_frames = copy(frame_part.at[1 - core], frame_in, 16, other_core)
+    swap_frames = copy(frame_part.at[1 - core], frame_in, 19, other_core)
     swap_frames.start()
     sent.extend([swap, swap_frames])
 
-    relay(0)
-    begin(far_copy(2))
-    relay(1)
-    begin(far_copy(3))
+    relay(2)
+    begin(near_copy(3))
+
+    swap.wait_recv()
+    layer_out[...] = small[core] + core_in[...]
+    swap_frames.wait_recv()
+    frame_pair[...] = frame_part[core] + frame_in[...]
+
+    def layer_copy(other, slot):
+        return pltpu.make_async_remote_copy(
+            src_ref=layer_out.at[other], dst_ref=layer_in.at[slot], send_sem=send_layer.at[0, other],
+            recv_sem=recv_layer.at[0, slot], device_id=at_z(other), device_id_type=MESH,
+        )
+
+    def frame_copy(other, slot):
+        return pltpu.make_async_remote_copy(
+            src_ref=frame_layer.at[z], dst_ref=frame_layer.at[slot], send_sem=send_layer.at[1, other],
+            recv_sem=recv_layer.at[1, slot], device_id=at_z(other), device_id_type=MESH,
+        )
+
+    for step in (4, 3, 5, 2, 6, 1, 7):
+        layer_copy(lax.rem(z + step, 8), z).start()
+    layer_in[z] = layer_out[z]
+    flip = copy(frame_pair.at[1 - y_hi], frame_other, 20, (lax.rem(space + 16, 32), tm))
+    begin(flip)
+
+    relay(3)
+    y_begin(0)
 
     rows_total = jnp.zeros((16, 160), f32)
     index_k = lax.broadcasted_iota(jnp.int32, (16, 256), 0)
@@ -317,98 +366,79 @@
         ones = (index_k == index_l + 2 * pair).astype(f32).astype(bf16)
         rows_total = rows_total + dot(ones, hi, NT) + dot(ones, lo, NT)
 
-    begin(near_copy(3))
-
-    swap.wait_recv()
-    layer_out[...] = small[core] + core_in[...]
-    swap_frames.wait_recv()
-    frame_layer[z] = frame_part[core] + frame_in[...]
-
-    def layer_copy(other, slot, kind):
-        if kind == 0:
-            source, target = layer_out.at[other], layer_in.at[slot]
-        else:
-            source, target = frame_layer.at[z], frame_layer.at[slot]
-        return pltpu.make_async_remote_copy(
-            src_ref=source, dst_ref=target, send_sem=send_layer.at[kind, other], recv_sem=recv_layer.at[kind, slot],
-            device_id=at_z(other), device_id_type=MESH,
-        )
+    y_begin(1)
+    relay(4)
+    begin(near_copy(5))
+    begin(near_copy(4))
+    relay(5)
+    y_begin(2)
+    unit_end(0)
+    y_begin(3)
+
+    flip.wait_recv()
+    frame_layer[z] = frame_pair[y_hi] + frame_other[...]
+    for step in (4, 3, 5, 2, 6, 1, 7):
+        frame_copy(lax.rem(z + step, 8), z).start()
 
     @pl.loop(1, 8)
     def _(step):
         other = lax.rem(z + step, 8)
-        layer_copy(other, z, 0).start()
-        layer_copy(other, z, 1).start()
-
-    layer_in[z] = layer_out[z]
-
-    y_begin(0)
-    relay(2)
-    begin(near_copy(4))
-    begin(after_copy(4))
-    y_begin(1)
-    relay(3)
-    begin(far_copy(4))
-    y_begin(2)
-
-    @pl.loop(1, 8)
-    def _(step):
-        other = lax.rem(z + step, 8)
-        layer_copy(other, other, 0).wait_recv()
-        layer_copy(other, other, 1).wait_recv()
+        layer_copy(other, other).wait_recv()
 
     line_out[0:40, :] = jnp.sum(layer_in[...], axis=0)
-    line_out[40:48, :] = rows_total[0:8, 0:128]
-    line_out[48:56, :] = jnp.concatenate([rows_total[0:8, 128:160], jnp.zeros((8, 96), f32)], axis=1)
-    frame_other[...] = jnp.sum(frame_layer[...], axis=0)
+    line_out[40:48, :] = jnp.zeros((8, 128), f32)
+    line_out[48:56, :] = rows_total[0:8, 0:128]
+    line_out[56:64, :] = jnp.concatenate([rows_total[0:8, 128:160], jnp.zeros((8, 96), f32)], axis=1)
 
     def line_copy(other, slot):
         return pltpu.make_async_remote_copy(
-            src_ref=line_out, dst_ref=line_in.at[slot], send_sem=send_line.at[other], recv_sem=recv_line.at[slot],
+            src_ref=line_out.at[pl.ds(pl.multiple_of(other * 16, 16), 16)], dst_ref=line_in.at[slot],
+            send_sem=send_line.at[other], recv_sem=recv_line.at[slot],
             device_id=at_x(other), device_id_type=MESH,
         )
 
-    for step in (1, 2, 3):
+    for step in (2, 1, 3):
         line_copy(lax.rem(x + step, 4), x).start()
-    line_in[x] = line_out[...]
-    flip = copy(frame_other, frame_last, 17, (lax.rem(space + 16, 32), tm))
-    flip.start()
-    sent.append(flip)
-
-    y_begin(3)
-    unit_end(0)
+    line_in[x] = line_out[pl.ds(pl.multiple_of(x * 16, 16), 16)]
+
     y_begin(4)
     unit_end(1)
+    unit_end(2)
 
     for step in (1, 2, 3):
         other = lax.rem(x + step, 4)
         line_copy(other, other).wait_recv()
-    summed = jnp.sum(line_in[...], axis=0)
-    for half in range(2):
-        ring_out[half, 0:16, :] = summed[16 * half : 16 * half + 16]
-        ring_out[half, 16:40, :] = summed[32:56]
+    ring_in[y] = jnp.sum(line_in[...], axis=0)
 
     def ring_copy(other, slot):
         return pltpu.make_async_remote_copy(
-            src_ref=ring_out.at[other // 4], dst_ref=ring_in.at[slot], send_sem=send_ring.at[other], recv_sem=recv_ring.at[slot],
+            src_ref=ring_in.at[y], dst_ref=ring_in.at[slot], send_sem=send_ring.at[other], recv_sem=recv_ring.at[slot],
             device_id=at_y(other), device_id_type=MESH,
         )
 
+    for step in (4, 3, 5, 2, 6, 1, 7):
+        ring_copy(lax.rem(y + step, 8), y).start()
+
+    unit_end(3)
+
     @pl.loop(1, 8)
     def _(step):
-        ring_copy(lax.rem(y + step, 8), y).start()
-
-    ring_in[y] = ring_out[y_hi]
-
-    flip.wait_recv()
-    frame_in_place = frame_other[...] + frame_last[...]
-    out_frames[core] = frame_in_place
-    swap_back = copy(out_frames.at[core], out_frames.at[core], 18, other_core)
-    swap_back.start()
-    sent.append(swap_back)
-
-    unit_end(2)
-    unit_end(3)
+        other = lax.rem(z + step, 8)
+        frame_copy(other, other).wait_recv()
+
+    out_frames[core, y_hi] = jnp.sum(frame_layer[...], axis=0)
+
+    def quarter_copy(device_core, device_half, slot_core, slot_half):
+        return pltpu.make_async_remote_copy(
+            src_ref=out_frames.at[core, y_hi], dst_ref=out_frames.at[slot_core, slot_half],
+            send_sem=send_quarter.at[device_core, device_half], recv_sem=recv_quarter.at[slot_core, slot_half],
+            device_id=(device_half * 16 + z * 2 + device_core, tm), device_id_type=MESH,
+        )
+
+    others = ((core, 1 - y_hi), (1 - core, 1 - y_hi), (1 - core, y_hi))
+    for other in others:
+        begin(quarter_copy(*other, core, y_hi))
+
     rest_end()
 
     mine = lax.rem(space, 16)
@@ -431,17 +461,17 @@
         other = lax.rem(y + step, 8)
         ring_copy(other, other).wait_recv()
 
-    final = jnp.sum(ring_in[:, 0:24, :], axis=0)
-    out_small[0:24, :] = final
-    out_small[24:40, :] = jnp.sum(ring_in[pl.ds(y_hi * 4, 4), 24:40, :], axis=0)
-
-    @pl.when(y_hi == 0)
-    def _():
-        out_small[16:24, 0:64] = final[16:24, 0:64]
-
-    @pl.when(y_hi == 1)
-    def _():
-        out_small[16:24, 0:64] = final[16:24, 64:128]
+    half_sum = jnp.sum(ring_in[pl.ds(y_hi * 4, 4)], axis=0)
+    piece_in[x] = jnp.where(x == 3, half_sum, jnp.sum(ring_in[...], axis=0))
+
+    def piece_copy(other, slot):
+        return pltpu.make_async_remote_copy(
+            src_ref=piece_in.at[x], dst_ref=piece_in.at[slot], send_sem=send_piece.at[other], recv_sem=recv_piece.at[slot],
+            device_id=at_x(other), device_id_type=MESH,
+        )
+
+    for step in (2, 1, 3):
+        piece_copy(lax.rem(x + step, 4), x).start()
 
     for each in sent:
         each.wait_send()
@@ -449,26 +479,40 @@
     @pl.loop(1, 8)
     def _(step):
         other = lax.rem(z + step, 8)
-        layer_copy(other, z, 0).wait_send()
-        layer_copy(other, z, 1).wait_send()
+        layer_copy(other, z).wait_send()
+        frame_copy(other, z).wait_send()
         other = lax.rem(y + step, 8)
         ring_copy(other, y).wait_send()
         for unit in range(5):
             y_copy(unit, other, y).wait_send()
 
     for step in (1, 2, 3):
-        line_copy(lax.rem(x + step, 4), x).wait_send()
+        other = lax.rem(x + step, 4)
+        line_copy(other, x).wait_send()
+        piece_copy(other, x).wait_send()
 
     @pl.loop(1, 16)
     def _(step):
         tile_copy(lax.rem(mine + step, 16), mine).wait_send()
+
+    for step in (1, 2, 3):
+        other = lax.rem(x + step, 4)
+        piece_copy(other, other).wait_recv()
+    out_small[0:16, :] = piece_in[y_hi]
+    out_small[16:24, :] = piece_in[2, 0:8]
+
+    @pl.when(y_hi == 1)
+    def _():
+        out_small[16:24, 0:64] = piece_in[2, 0:8, 64:128]
+
+    out_small[24:40, :] = piece_in[3]
+    for other in others:
+        quarter_copy(*other, *other).wait_recv()
 
     @pl.loop(1, 16)
     def _(step):
         other = lax.rem(mine + step, 16)
         tile_copy(other, other).wait_recv()
-
-    swap_back.wait_recv()
 
 
 def finish(gathered, small, frames, core_rows, out_rows, out_cols, out_frames, out_core):
@@ -508,18 +552,18 @@
         pltpu.VMEM((256, 128), f32),
         pltpu.VMEM((2, 8, 40, 128), f32), pltpu.VMEM((8, 40, 128), f32),
         pltpu.VMEM((8, 40, 128), f32), pltpu.VMEM((8, 40, 128), f32),
-        pltpu.VMEM((2, 48, 128), f32), pltpu.VMEM((48, 128), f32), pltpu.VMEM((8, 48, 128), f32),
-        pltpu.VMEM((48, 128), f32), pltpu.VMEM((48, 128), f32),
-        pltpu.VMEM((56, 128), f32), pltpu.VMEM((4, 56, 128), f32),
-        pltpu.VMEM((2, 40, 128), f32), pltpu.VMEM((8, 40, 128), f32),
-        dma((12,)), dma((20,)), dma((20,)), dma((16,)), dma((16,)), dma((2, 8)), dma((2, 8)), dma((4,)), dma((4,)), dma((8,)), dma((8,)), dma((5, 8)), dma((5, 8)),
+        pltpu.VMEM((2, 2, 24, 128), f32), pltpu.VMEM((2, 24, 128), f32), pltpu.VMEM((2, 24, 128), f32),
+        pltpu.VMEM((24, 128), f32), pltpu.VMEM((8, 24, 128), f32),
+        pltpu.VMEM((64, 128), f32), pltpu.VMEM((4, 16, 128), f32), pltpu.VMEM((8, 16, 128), f32), pltpu.VMEM((4, 16, 128), f32),
+        dma((12,)), dma((22,)), dma((22,)), dma((16,)), dma((16,)), dma((2, 8)), dma((2, 8)), dma((4,)), dma((4,)), dma((8,)), dma((8,)), dma((5, 8)), dma((5, 8)),
+        dma((4,)), dma((4,)), dma((2, 2)), dma((2, 2)),
     ]
     gathered, small, frames = pl.pallas_call(
         kernel,
         out_shape=[
             jax.ShapeDtypeStruct((2, 16, 8, 128), f32),
             jax.ShapeDtypeStruct((40, 128), f32),
-            jax.ShapeDtypeStruct((2, 48, 128), f32),
+            jax.ShapeDtypeStruct((2, 2, 24, 128), f32),
         ],
         in_specs=[pl.BlockSpec(memory_space=pltpu.HBM)] * 9,
         out_specs=[vmem] * 3,
@@ -531,7 +575,7 @@
         out_shape=[
             jax.ShapeDtypeStruct((8, 160), f32),
             jax.ShapeDtypeStruct((16, 160), f32),
-            jax.ShapeDtypeStruct((2, 48, 128), f32),
+            jax.ShapeDtypeStruct((2, 2, 24, 128), f32),
             jax.ShapeDtypeStruct((10, 12, 320), f32),
         ],
         in_specs=[vmem] * 4,

time: 54.8 us -> 51.2 us (0.934)
  Pallas kernels: 54.1 us -> 50.4 us
    pallas_call x1, Pallas kernels: 51.9 us -> 48.2 us  [per_device(): pl.pallas_call(kernel, out_shape=[jax.ShapeDtypeStruct((2, 16, 8, 128), f...]
where the time goes in v3:
time: 51.2 us; the launch traced here: 51 us
  Pallas kernels  50.4 us (98%)
  between operations  0.64 us (1%)
    pallas_call x1, Pallas kernels, per_device(): pl.pallas_call(kernel, out_shape=[jax.ShapeDtypeStruct((2, 16, 8, 128), f...  48.2 us
    pallas_call x1, Pallas kernels, per_device(): pl.pallas_call(finish, out_shape=[jax.ShapeDtypeStruct((8, 160), f32), ja...  2.16 us

profile of v3, /device:TPU:1, one launch (start us, length us, event | category | flops | bytes accessed | tf_op | source)
XLA Modules:
  0.0 51.0 jit_solution(1797512087325485966)
XLA Ops:
  0.6 48.2 %shard_map.129 = (f32[2,16,8,128]{3,2,1,0:T(8,128)}, f32[40,128]{1,0:T(8,128)}, f32[2,2,24,128]{3,2,1,0:T(8,128)}) custom-call(f32[8,512,128]{2,1,0:T(8,128)} %slab_given.1, f32[160,512]{1,0:T(8,128)} %bitcast.13, f32[96,512]{1,0:T(8,128)} %bitcast.14, f32[320,512]{1,0:T(8,128)} %bitcast.11, f32[160,128]{1,0:T(8,128)} %bitcast.16, f32[160,128]{1,0:T(8,128)} %bitcast.17, ...), custom_call_target="tpu_custom_call" | custom-call | tf_op jit(solution)/shard_map/pallas_call | solution.py:561
  48.9 2.2 %shard_map.130 = (f32[8,160]{1,0:T(8,128)}, f32[16,160]{1,0:T(8,128)}, f32[2,2,24,128]{3,2,1,0:T(8,128)}, f32[10,12,320]{2,1,0:T(8,128)}) custom-call(f32[2,16,8,128]{3,2,1,0:T(8,128)} %get-tuple-element.11.gathered, f32[40,128]{1,0:T(8,128)} %get-tuple-element.12.small, f32[2,2,24,128]{3,2,1,0:T(8,128)} %get-tuple-element.13.frames, f32[320,256]{1,0:T(8,128)} %bitcast.12), custom_call_target="tpu_custom_call" | custom-call | tf_op jit(solution)/shard_map/pallas_call | solution.py:573

commit v4 on v3

--- a/solution.py
+++ b/solution.py
@@ -28,6 +28,7 @@
     slab_given, first_cols_given, third_cols_given, core_cols_given, first_frames_given, second_frames_given,
     core_frames_given, second_rows_given, third_rows_given,
     gathered, out_small, out_frames,
+    small_sums, frame_sums,
     slab, first_cols, third_cols, core_cols, first_frames, second_frames, core_frames, second_rows, third_rows,
     order, cols_hi, cols_lo, frames_hi, frames_lo, split, inner, rest_hi, rest_lo, second_hi, second_lo, third_wide,
     part, far, near, after, line, tiles,
@@ -366,13 +367,12 @@
         ones = (index_k == index_l + 2 * pair).astype(f32).astype(bf16)
         rows_total = rows_total + dot(ones, hi, NT) + dot(ones, lo, NT)
 
-    y_begin(1)
-    relay(4)
     begin(near_copy(5))
     begin(near_copy(4))
+    relay(4)
+    y_begin(1)
     relay(5)
     y_begin(2)
-    unit_end(0)
     y_begin(3)
 
     flip.wait_recv()
@@ -402,6 +402,7 @@
     line_in[x] = line_out[pl.ds(pl.multiple_of(x * 16, 16), 16)]
 
     y_begin(4)
+    unit_end(0)
     unit_end(1)
     unit_end(2)
 
@@ -426,11 +427,11 @@
         other = lax.rem(z + step, 8)
         frame_copy(other, other).wait_recv()
 
-    out_frames[core, y_hi] = jnp.sum(frame_layer[...], axis=0)
+    frame_sums[core, y_hi] = jnp.sum(frame_layer[...], axis=0)
 
     def quarter_copy(device_core, device_half, slot_core, slot_half):
         return pltpu.make_async_remote_copy(
-            src_ref=out_frames.at[core, y_hi], dst_ref=out_frames.at[slot_core, slot_half],
+            src_ref=frame_sums.at[core, y_hi], dst_ref=frame_sums.at[slot_core, slot_half],
             send_sem=send_quarter.at[device_core, device_half], recv_sem=recv_quarter.at[slot_core, slot_half],
             device_id=(device_half * 16 + z * 2 + device_core, tm), device_id_type=MESH,
         )
@@ -454,7 +455,8 @@
     for step in (8, 7, 9, 6, 10, 5, 11, 4, 12, 3, 13, 2, 14, 1, 15):
         tile_copy(lax.rem(mine + step, 16), mine).start()
 
-    gathered[:, mine] = tile_view[mine]
+    keep = load(0, tile_view.at[mine], gathered.at[:, mine])
+    keep.start()
 
     @pl.loop(1, 8)
     def _(step):
@@ -498,21 +500,28 @@
     for step in (1, 2, 3):
         other = lax.rem(x + step, 4)
         piece_copy(other, other).wait_recv()
-    out_small[0:16, :] = piece_in[y_hi]
-    out_small[16:24, :] = piece_in[2, 0:8]
+    small_sums[0:16, :] = piece_in[y_hi]
+    small_sums[16:24, :] = piece_in[2, 0:8]
 
     @pl.when(y_hi == 1)
     def _():
-        out_small[16:24, 0:64] = piece_in[2, 0:8, 64:128]
-
-    out_small[24:40, :] = piece_in[3]
+        small_sums[16:24, 0:64] = piece_in[2, 0:8, 64:128]
+
+    small_sums[24:40, :] = piece_in[3]
+    keep_small = load(1, small_sums, out_small)
+    keep_small.start()
     for other in others:
         quarter_copy(*other, *other).wait_recv()
+    keep_frames = load(2, frame_sums, out_frames)
+    keep_frames.start()
 
     @pl.loop(1, 16)
     def _(step):
         other = lax.rem(mine + step, 16)
         tile_copy(other, other).wait_recv()
+
+    for each in (keep, keep_small, keep_frames):
+        each.wait()
 
 
 def finish(gathered, small, frames, core_rows, out_rows, out_cols, out_frames, out_core):
@@ -538,7 +547,8 @@
     )
     vmem = pl.BlockSpec(memory_space=pltpu.VMEM)
     dma = pltpu.SemaphoreType.DMA
-    scratch = [pltpu.VMEM(each.shape, f32) for each in arguments] + [
+    scratch = [pltpu.VMEM((40, 128), f32), pltpu.VMEM((2, 2, 24, 128), f32)]
+    scratch += [pltpu.VMEM(each.shape, f32) for each in arguments] + [
         pltpu.VMEM((4, 320, 128), f32),
         pltpu.VMEM((576, 512), bf16), pltpu.VMEM((576, 512), bf16),
         pltpu.VMEM((384, 256), bf16), pltpu.VMEM((384, 256), bf16),
@@ -566,7 +576,7 @@
             jax.ShapeDtypeStruct((2, 2, 24, 128), f32),
         ],
         in_specs=[pl.BlockSpec(memory_space=pltpu.HBM)] * 9,
-        out_specs=[vmem] * 3,
+        out_specs=[pl.BlockSpec(memory_space=pltpu.HBM)] * 3,
         scratch_shapes=scratch,
         compiler_params=pltpu.CompilerParams(collective_id=0, has_side_effects=True, vmem_limit_bytes=60 * 2**20),
     )(*arguments)

time: 51.2 us -> 50.2 us (0.980)
  Pallas kernels: 50.4 us -> 49.4 us
    pallas_call x1, Pallas kernels: 48.2 us -> 47.2 us  [per_device(): pl.pallas_call(kernel, out_shape=[jax.ShapeDtypeStruct((2, 16, 8, 128), f...]
where the time goes in v4:
time: 50.2 us; the launch traced here: 50 us
  Pallas kernels  49.4 us (98%)
  between operations  0.64 us (1%)
    pallas_call x1, Pallas kernels, per_device(): pl.pallas_call(kernel, out_shape=[jax.ShapeDtypeStruct((2, 16, 8, 128), f...  47.2 us
    pallas_call x1, Pallas kernels, per_device(): pl.pallas_call(finish, out_shape=[jax.ShapeDtypeStruct((8, 160), f32), ja...  2.16 us

profile of v4, /device:TPU:1, one launch (start us, length us, event | category | flops | bytes accessed | tf_op | source)
XLA Modules:
  0.0 50.0 jit_solution(2351410525286269654)
XLA Ops:
  0.6 47.2 %shard_map.129 = (f32[2,16,8,128]{3,2,1,0:T(8,128)}, f32[40,128]{1,0:T(8,128)}, f32[2,2,24,128]{3,2,1,0:T(8,128)}) custom-call(f32[8,512,128]{2,1,0:T(8,128)} %slab_given.1, f32[160,512]{1,0:T(8,128)} %bitcast.13, f32[96,512]{1,0:T(8,128)} %bitcast.14, f32[320,512]{1,0:T(8,128)} %bitcast.11, f32[160,128]{1,0:T(8,128)} %bitcast.16, f32[160,128]{1,0:T(8,128)} %bitcast.17, ...), custom_call_target="tpu_custom_call" | custom-call | tf_op jit(solution)/shard_map/pallas_call | solution.py:571
  47.9 2.2 %shard_map.130 = (f32[8,160]{1,0:T(8,128)}, f32[16,160]{1,0:T(8,128)}, f32[2,2,24,128]{3,2,1,0:T(8,128)}, f32[10,12,320]{2,1,0:T(8,128)}) custom-call(f32[2,16,8,128]{3,2,1,0:T(8,128)} %get-tuple-element.11.gathered, f32[40,128]{1,0:T(8,128)} %get-tuple-element.12.small, f32[2,2,24,128]{3,2,1,0:T(8,128)} %get-tuple-element.13.frames, f32[320,256]{1,0:T(8,128)} %bitcast.12), custom_call_target="tpu_custom_call" | custom-call | tf_op jit(solution)/shard_map/pallas_call | solution.py:583

commit v5 on v4

--- a/solution.py
+++ b/solution.py
@@ -193,7 +193,7 @@
     def y_copy(unit, other, slot):
         return pltpu.make_async_remote_copy(
             src_ref=part.at[unit, x, other // 4, lax.rem(other, 4)], dst_ref=line.at[unit, slot],
-            send_sem=send_y.at[unit, other], recv_sem=recv_y.at[unit, slot],
+            send_sem=send_y.at[unit, other], recv_sem=recv_y.at[unit],
             device_id=at_y(other), device_id_type=MESH,
         )
 
@@ -218,11 +218,8 @@
     lane_place = lax.rem(lane_place, 128) // 12
 
     def y_end(unit):
-        @pl.loop(1, 8)
-        def _(step):
-            other = lax.rem(y + step, 8)
-            y_copy(unit, other, other).wait_recv()
-
+        all_seven = line.at[unit, pl.ds(0, 7)]
+        pltpu.make_async_copy(all_seven, all_seven, recv_y.at[unit]).wait()
         value = jnp.concatenate([jnp.sum(line[unit, 0:4], axis=0), jnp.sum(line[unit, 4:8], axis=0)], axis=1)
         turned = dot(jnp.concatenate(halves(value), axis=0), pick, TN)
         return turned.reshape(2, 8, 16, 256)
@@ -448,7 +445,7 @@
     def tile_copy(other, slot):
         return pltpu.make_async_remote_copy(
             src_ref=tile_view.at[other], dst_ref=gathered.at[:, slot],
-            send_sem=send_space.at[other], recv_sem=recv_space.at[slot],
+            send_sem=send_space.at[other], recv_sem=recv_space.at[0],
             device_id=(y_hi * 16 + other, tm), device_id_type=MESH,
         )
 
@@ -515,10 +512,8 @@
     keep_frames = load(2, frame_sums, out_frames)
     keep_frames.start()
 
-    @pl.loop(1, 16)
-    def _(step):
-        other = lax.rem(mine + step, 16)
-        tile_copy(other, other).wait_recv()
+    all_fifteen = gathered.at[:, pl.ds(0, 15)]
+    pltpu.make_async_copy(all_fifteen, all_fifteen, recv_space.at[0]).wait()
 
     for each in (keep, keep_small, keep_frames):
         each.wait()
@@ -565,7 +560,7 @@
         pltpu.VMEM((2, 2, 24, 128), f32), pltpu.VMEM((2, 24, 128), f32), pltpu.VMEM((2, 24, 128), f32),
         pltpu.VMEM((24, 128), f32), pltpu.VMEM((8, 24, 128), f32),
         pltpu.VMEM((64, 128), f32), pltpu.VMEM((4, 16, 128), f32), pltpu.VMEM((8, 16, 128), f32), pltpu.VMEM((4, 16, 128), f32),
-        dma((12,)), dma((22,)), dma((22,)), dma((16,)), dma((16,)), dma((2, 8)), dma((2, 8)), dma((4,)), dma((4,)), dma((8,)), dma((8,)), dma((5, 8)), dma((5, 8)),
+        dma((12,)), dma((22,)), dma((22,)), dma((16,)), dma((1,)), dma((2, 8)), dma((2, 8)), dma((4,)), dma((4,)), dma((8,)), dma((8,)), dma((5, 8)), dma((5,)),
         dma((4,)), dma((4,)), dma((2, 2)), dma((2, 2)),
     ]
     gathered, small, frames = pl.pallas_call(

time: 50.2 us -> 49.7 us (0.990)
  no operation moved by 1% of the time
where the time goes in v5:
time: 49.7 us; the launch traced here: 49.6 us
  Pallas kernels  48.9 us (98%)
  between operations  0.64 us (1%)
    pallas_call x1, Pallas kernels, per_device(): pl.pallas_call(kernel, out_shape=[jax.ShapeDtypeStruct((2, 16, 8, 128), f...  46.8 us
    pallas_call x1, Pallas kernels, per_device(): pl.pallas_call(finish, out_shape=[jax.ShapeDtypeStruct((8, 160), f32), ja...  2.16 us

profile of v5, /device:TPU:1, one launch (start us, length us, event | category | flops | bytes accessed | tf_op | source)
XLA Modules:
  0.0 49.6 jit_solution(15555434215767950757)
XLA Ops:
  0.6 46.8 %shard_map.129 = (f32[2,16,8,128]{3,2,1,0:T(8,128)}, f32[40,128]{1,0:T(8,128)}, f32[2,2,24,128]{3,2,1,0:T(8,128)}) custom-call(f32[8,512,128]{2,1,0:T(8,128)} %slab_given.1, f32[160,512]{1,0:T(8,128)} %bitcast.13, f32[96,512]{1,0:T(8,128)} %bitcast.14, f32[320,512]{1,0:T(8,128)} %bitcast.11, f32[160,128]{1,0:T(8,128)} %bitcast.16, f32[160,128]{1,0:T(8,128)} %bitcast.17, ...), custom_call_target="tpu_custom_call" | custom-call | tf_op jit(solution)/shard_map/pallas_call | solution.py:566
  47.4 2.2 %shard_map.130 = (f32[8,160]{1,0:T(8,128)}, f32[16,160]{1,0:T(8,128)}, f32[2,2,24,128]{3,2,1,0:T(8,128)}, f32[10,12,320]{2,1,0:T(8,128)}) custom-call(f32[2,16,8,128]{3,2,1,0:T(8,128)} %get-tuple-element.11.gathered, f32[40,128]{1,0:T(8,128)} %get-tuple-element.12.small, f32[2,2,24,128]{3,2,1,0:T(8,128)} %get-tuple-element.13.frames, f32[320,256]{1,0:T(8,128)} %bitcast.12), custom_call_target="tpu_custom_call" | custom-call | tf_op jit(solution)/shard_map/pallas_call | solution.py:578
